TPU v7x, 32 devices: a whole 2x2x4 slice. The times are simulated.
32 devices in a mesh: groups: 2 (over x), tensor: 16 (over z, y, core).
Axes of the slice: x: 2, y: 2, z: 4, core: 2. Of those that a mesh axis runs over, the one named last changes fastest.
Arguments:
- hidden_in: bfloat16 [256, 8192], P('groups', 'tensor'), parts along dimension 0, may hold values from -6 to 6
- norm_gain: bfloat16 [8192], replicated, may hold values from 0.099609375 to 1.8984375
- query_base_matrix: bfloat16 [8192, 8192], P(None, 'tensor'), may hold values from -0.0625 to 0.0625
- kv_weight: bfloat16 [8192, 2048], P('tensor'), may hold values from -0.0625 to 0.0625
- out_weight: bfloat16 [8192, 8192], P('tensor'), may hold values from -0.09375 to 0.09375
- query_down: bfloat16 [16, 8192, 64], P('tensor'), may hold values from -0.0625 to 0.0625
- query_up_factor: bfloat16 [16, 64, 8192], P('tensor'), may hold values from -0.75 to 0.75
- output_down: bfloat16 [16, 8192, 64], P('tensor'), may hold values from -0.0625 to 0.0625
- output_up_factor: bfloat16 [16, 64, 8192], P('tensor'), may hold values from -0.75 to 0.75
- variant_ids: int32 [256, 1], P('groups'), parts along dimension 0, may hold values from 0 to 15
- cache_lengths: int32 [256], P('groups'), parts along dimension 0, may hold values from 1 to 16, 1280 in all
- kv_cache: bfloat16 [16, 256, 16, 256], P('tensor', 'groups'), parts along dimension 1, as said below
Outputs:
- projected: bfloat16 [256, 8192], P('groups', 'tensor'), parts along dimension 0
There are 2 independent parts, one for each index of `groups`. A program takes and returns all parts, laid end to end along the dimension named above; an argument that names none is the same for every part. Nothing has to cross between parts.
Inputs may be any that keep to these rules, and one draw needn't show every extreme that they name: `variant_ids`: every one of the 16 variants is named by at least one row. `kv_cache`: the 2 copies of one key-value head are identical: copy c equals copy c2 whenever c // 2 == c2 // 2.
All inputs are finite; a program needn't handle non-finite values.
Results may differ from a plain program's by a relative error of at most 0.012.
The roundings to bfloat16 on the way count: a program that leaves them out, or rounds other values in their place, can miss the bound.
Values may be sent and summed in bfloat16 or wider, within the bound.
A program may use at most 128 MiB of HBM per device.

v0:
```python
import jax
import jax.numpy as jnp
from jax import lax
from jax.sharding import PartitionSpec as P

H = 64
KVH = 8
HD = 128


adapter_scale = 2.0


def body(
    hidden_in,
    norm_gain,
    query_base_matrix,
    kv_weight,
    out_weight,
    query_down,
    query_up_factor,
    output_down,
    output_up_factor,
    variant_ids,
    cache_lengths,
    kv_cache,
):
    shard = lax.axis_index("tensor")
    shards = lax.axis_size("tensor")
    whole = lax.all_gather(hidden_in, "tensor", axis=1, tiled=True)
    wide = whole.astype(jnp.float32)
    normalized_input = (
        wide
        * lax.rsqrt(jnp.mean(wide * wide, axis=1, keepdims=True) + 1e-06)
        * norm_gain.astype(jnp.float32)
    ).astype(jnp.bfloat16)
    rows_total = normalized_input.shape[0]
    slab = kv_weight.shape[0]
    own_columns = lax.dynamic_slice_in_dim(normalized_input, shard * slab, slab, 1)
    kv_part = jnp.dot(own_columns, kv_weight, preferred_element_type=jnp.float32)
    held = query_down.shape[0]
    variants_all = held * shards
    mine = shard * held + jnp.arange(held, dtype=jnp.int32)
    picked_variants = variant_ids[:, 0]
    owned = picked_variants[:, None] == mine[None, :]
    local_factor = jnp.einsum(
        "rd,jdk->rjk", normalized_input, query_down, preferred_element_type=jnp.float32
    )
    catalog = jnp.arange(variants_all, dtype=jnp.int32)
    onehot = (picked_variants[:, None] == catalog[None, :]).astype(jnp.bfloat16)
    query_base_part = jnp.dot(
        normalized_input, query_base_matrix, preferred_element_type=jnp.float32
    )
    fresh_sum = lax.psum(kv_part, "tensor")
    masked = jnp.where(owned[:, :, None], local_factor, 0.0).astype(jnp.bfloat16)
    query_delta_part = lax.psum_scatter(
        jnp.einsum("jkc,rjk->cr", query_up_factor, masked, preferred_element_type=jnp.float32),
        "tensor",
        scatter_dimension=0,
        tiled=True,
    ).T
    query_vectors = (query_base_part + adapter_scale * query_delta_part).astype(jnp.bfloat16)
    fresh = fresh_sum.astype(jnp.bfloat16)
    local_heads = query_base_matrix.shape[1] // HD
    group = H // KVH
    kv_head = shard * local_heads // group
    fresh_head = lax.dynamic_slice_in_dim(fresh, kv_head * 2 * HD, 2 * HD, 1)
    fresh_key = fresh_head[:, :HD]
    fresh_value = fresh_head[:, HD:]
    query_heads = query_vectors.reshape(rows_total, local_heads, HD)
    stored = kv_cache[0]
    keys = stored[:, :, :HD]
    values = stored[:, :, HD:]
    scale = 1.0 / HD**0.5
    scores = (
        jnp.einsum("rhd,rld->rhl", query_heads, keys, preferred_element_type=jnp.float32) * scale
    )
    own = (
        jnp.einsum("rhd,rd->rh", query_heads, fresh_key, preferred_element_type=jnp.float32) * scale
    )
    positions = jnp.arange(stored.shape[1], dtype=jnp.int32)
    live = positions[None, :] < cache_lengths[:, None]
    scores = jnp.where(live[:, None, :], scores, -jnp.inf)
    top = jnp.maximum(jnp.max(scores, axis=2), own)
    expo = jnp.exp(scores - top[:, :, None])
    own_expo = jnp.exp(own - top)
    total = jnp.sum(expo, axis=2) + own_expo
    weights = (expo / total[:, :, None]).astype(jnp.bfloat16)
    own_weight = (own_expo / total).astype(jnp.bfloat16)
    mixed_heads = jnp.einsum("rhl,rld->rhd", weights, values, preferred_element_type=jnp.float32)
    mixed_heads = (
        mixed_heads
        + own_weight.astype(jnp.float32)[:, :, None] * fresh_value.astype(jnp.float32)[:, None, :]
    )
    attended = mixed_heads.astype(jnp.bfloat16).reshape(rows_total, local_heads * HD)
    factor_panels = lax.all_to_all(output_down, "tensor", split_axis=1, concat_axis=0, tiled=True)
    per_variant = jnp.einsum(
        "rc,vck->rvk", attended, factor_panels, preferred_element_type=jnp.float32
    )
    factor_part = jnp.sum(onehot.astype(jnp.float32)[:, :, None] * per_variant, axis=1)
    output_factor_rows = lax.psum(factor_part, "tensor").astype(jnp.bfloat16)
    summed_result = lax.psum_scatter(
        lax.dot_general(
            out_weight, attended, (((0,), (1,)), ((), ())), preferred_element_type=jnp.float32
        ),
        "tensor",
        scatter_dimension=0,
        tiled=True,
    ).T
    up_panels = lax.all_to_all(output_up_factor, "tensor", split_axis=2, concat_axis=0, tiled=True)
    spread_o = onehot[:, :, None] * output_factor_rows[:, None, :]
    delta_product = jnp.einsum(
        "rvk,vkc->rc", spread_o, up_panels, preferred_element_type=jnp.float32
    )
    projected = (summed_result + adapter_scale * delta_product).astype(jnp.bfloat16)
    return projected


def solution(mesh):
    in_specs = (
        P("groups", "tensor"),
        P(),
        P(None, "tensor"),
        P("tensor", None),
        P("tensor", None),
        P("tensor", None, None),
        P("tensor", None, None),
        P("tensor", None, None),
        P("tensor", None, None),
        P("groups", None),
        P("groups"),
        P("tensor", "groups", None, None),
    )
    out_specs = P("groups", "tensor")
    return jax.shard_map(body, mesh=mesh, in_specs=in_specs, out_specs=out_specs, check_vma=False)
```

profile of v0, /device:TPU:0, one launch (start us, length us, event | category | flops | bytes accessed | tf_op | source)
XLA Modules:
  0.0 393.0 jit_solution(15297688398879093812)
XLA Ops:
  6.5 0.7 all-gather.2.cloned.1.call-update
  7.3 0.7 convert_element_type.58
  8.0 0.7 compare_bitcast_fusion
  8.7 44.7 %all-gather.2.cloned.1.call-done = bf16[128,8192]{1,0:T(8,128)(2,1)} async-done(((bf16[128,512]{1,0:T(8,128)(2,1)}), bf16[128,8192]{1,0:T(8,128)(2,1)}) %all-gather.2.cloned.1.call-update) | async-done | bytes 2097168 | tf_op jit(solution)/shard_map/all_gather | solution.py:30
  53.4 2.1 fusion
  55.5 3.5 fusion.2
  59.0 6.3 %convolution_bitcast_fusion.1 = f32[8192,128]{0,1:T(8,128)} fusion(bf16[128,8192]{1,0:T(8,128)(2,1)} %fusion.2, bf16[1,64,8192]{2,1,0:T(8,128)(2,1)S(1)} %copy-done.2, bf16[1,8192,64]{1,2,0:T(8,128)(2,1)} %param.17, pred[128]{0:T(512)(128)(4,1)S(1)} %compare_bitcast_fusion), kind=kOutput, calls=%fused_computation.1 | convolution fusion | flops 268451840 | bytes 8388736 | tf_op jit(solution)/shard_map/jkc,rjk->cr/dot_general | solution.py:57
  65.4 0.6 copy-done.4
  66.0 1.4 fusion.25
  67.4 76.3 %all-reduce.1 = bf16[128,2048]{1,0:T(8,128)(2,1)S(1)} all-reduce(f32[128,2048]{1,0:T(8,128)S(1)} %fusion.25), channel_id=1, replica_groups=mesh['groups'=2,'tensor'=16] {'tensor'}, use_global_device_ids=true, to_apply=%region_3.4 | all-reduce | flops 262144 | bytes 1572864 | tf_op jit(solution)/shard_map/psum | solution.py:54
  144.2 5.2 %fusion.6 = bf16[128,512]{1,0:T(8,128)(2,1)S(1)} fusion(bf16[128,8192]{1,0:T(8,128)(2,1)} %fusion.2, bf16[8192,512]{1,0:T(8,128)(2,1)} %param.14, f32[512,128]{0,1:T(8,128)} %reduce-scatter.3.cloned.1.call-done), kind=kOutput, calls=%fused_computation.14 | convolution fusion | flops 1073938432 | bytes 10878976 | tf_op jit(solution)/shard_map/dot_general | solution.py:51
  151.7 6.6 %convolution_bitcast_fusion = f32[8192,128]{0,1:T(8,128)} fusion(bf16[512,8192]{1,0:T(8,128)(2,1)} %param.16, bf16[16,8,4,128]{3,2,1,0:T(4,128)(2,1)S(1)} %bitcast.82), kind=kOutput, calls=%fused_computation | convolution fusion | flops 1073741824 | bytes 12713984 | tf_op jit(solution)/shard_map/dot_general | solution.py:103
  158.3 1.2 copy-done.3
  159.5 6.8 %copy.40 = bf16[1,8192,64]{2,0,1:T(2,128)(2,1)} copy(bf16[1,8192,64]{1,2,0:T(8,128)(2,1)S(1)} %copy-done.3) | data formatting | bytes 2097152 | tf_op args[7]
  166.3 0.5 broadcast.70
  166.8 45.3 %reduce.1 = bf16[8192,64]{1,0:T(8,128)(2,1)S(1)} reduce(bf16[8192,1,64]{2,1,0:T(2,128)(2,1)} %bitcast.74, bf16[]{:T(256)} %broadcast.70), dimensions={1}, to_apply=%bitcast.64.reduce_sub_computation | reduce | bytes 2097154
  212.1 2.3 reshape.114
  214.4 3.9 all-to-all-start
  218.3 9.2 %copy.43 = bf16[1,64,8192]{1,0,2:T(2,128)(2,1)} copy(bf16[1,64,8192]{2,1,0:T(8,128)(2,1)} %param.20) | data formatting | bytes 2097152 | tf_op args[8]
  227.5 45.2 %reduce = bf16[8192,64]{1,0:T(8,128)(2,1)S(1)} reduce(bf16[8192,1,64]{2,1,0:T(2,128)(2,1)} %bitcast.75, bf16[]{:T(256)} %broadcast.70), dimensions={1}, to_apply=%bitcast.62.reduce_sub_computation | reduce | bytes 2097154
  272.7 2.2 reshape.112
  275.0 5.8 %all-to-all-start.1 = ((bf16[16,2,16384]{2,1,0:T(2,128)(2,1)}), bf16[16,2,16384]{2,1,0:T(2,128)(2,1)}, u32[]{:S(2)}, u32[]{:S(2)}) async-start(bf16[16,2,16384]{2,1,0:T(2,128)(2,1)} %reshape.112), calls=%async_computation.3 | async-start | bytes 2097152 | tf_op jit(solution)/shard_map/all_to_all | solution.py:110
  280.8 7.0 %reshape.115 = bf16[8192,1,64]{2,1,0:T(2,128)(2,1)} reshape(bf16[16,2,16384]{2,1,0:T(2,128)(2,1)S(1)} %all-to-all-done) | data formatting | bytes 2097152
  287.8 2.5 copy.52
  290.3 1.6 copy.42
  291.9 11.9 %all-to-all-done.1 = bf16[16,2,16384]{2,1,0:T(2,128)(2,1)} async-done(((bf16[16,2,16384]{2,1,0:T(2,128)(2,1)}), bf16[16,2,16384]{2,1,0:T(2,128)(2,1)}, u32[]{:S(2)}, u32[]{:S(2)}) %all-to-all-start.1) | async-done | bytes 1048608 | tf_op jit(solution)/shard_map/all_to_all | solution.py:110
  303.8 10.2 %reshape.113 = bf16[8192,1,64]{2,1,0:T(2,128)(2,1)} reshape(bf16[16,2,16384]{2,1,0:T(2,128)(2,1)} %all-to-all-done.1) | data formatting | bytes 2097152
  314.0 4.0 %copy.53 = bf16[1,64,8192]{1,2,0:T(8,128)(2,1)} copy(bf16[1,64,8192]{1,0,2:T(2,128)(2,1)} %bitcast.77) | data formatting | bytes 2097152
  318.0 1.9 copy.45
  319.9 1.7 fusion.18
  321.6 62.9 %psum.15 = bf16[128,64]{0,1:T(8,128)(2,1)S(1)} all-reduce(f32[128,64]{0,1:T(8,128)S(1)} %multiply_reduce_fusion), channel_id=1, replica_groups=mesh['groups'=2,'tensor'=16] {'tensor'}, use_global_device_ids=true, to_apply=%region_7.8 | all-reduce | flops 8192 | bytes 49152 | tf_op jit(solution)/shard_map/psum | solution.py:101
  384.5 1.9 fusion.8
  (39 shorter events, 3.0 us)
Async XLA Ops:
  6.5 59.5 %copy-start = (bf16[512,2048]{1,0:T(8,128)(2,1)S(1)}, bf16[512,2048]{1,0:T(8,128)(2,1)}, u32[]{:S(2)}) copy-start(bf16[512,2048]{1,0:T(8,128)(2,1)} %param.15) | copy-start | bytes 6291460
  6.5 52.5 %copy-start.2 = (bf16[1,64,8192]{2,1,0:T(8,128)(2,1)S(1)}, bf16[1,64,8192]{2,1,0:T(8,128)(2,1)}, u32[]{:S(2)}) copy-start(bf16[1,64,8192]{2,1,0:T(8,128)(2,1)} %param.18) | copy-start | bytes 3145732
  6.5 46.9 %all-gather.2.cloned.1.call-start = ((), (), s32[]{:S(2)}) async-start(), calls=%async_computation.4 | async-start | bytes 2228224 | tf_op jit(solution)/shard_map/all_gather | solution.py:30
  7.3 136.9 %reduce-scatter.3.cloned.1.call-start = ((), (), s32[]{:S(2)}) async-start(), calls=%async_computation.5 | async-start | bytes 4456448 | tf_op jit(solution)/shard_map/reduce_scatter | solution.py:56
  65.3 0.7 copy-start.4
  65.3 319.2 %reduce-scatter.5.cloned.1.call-start = ((), (), s32[]{:S(2)}) async-start(), calls=%async_computation.6 | async-start | bytes 4456448 | tf_op jit(solution)/shard_map/reduce_scatter | solution.py:102
  143.7 6.1 %copy-start.6 = (bf16[1,128,16,256]{3,2,1,0:T(8,128)(2,1)S(1)}, bf16[1,128,16,256]{3,2,1,0:T(8,128)(2,1)}, u32[]{:S(2)}) copy-start(bf16[1,128,16,256]{3,2,1,0:T(8,128)(2,1)} %param.23) | copy-start | bytes 3145732
  158.3 1.2 copy-start.3
  214.4 60.6 %all-to-all-start = ((bf16[16,2,16384]{2,1,0:T(2,128)(2,1)}), bf16[16,2,16384]{2,1,0:T(2,128)(2,1)S(1)}, u32[]{:S(2)}, u32[]{:S(2)}) async-start(bf16[16,2,16384]{2,1,0:T(2,128)(2,1)} %reshape.114), calls=%async_computation.2 | async-start | bytes 2097152 | tf_op jit(solution)/shard_map/all_to_all | solution.py:96
  272.7 8.1 %copy-start.5 = (s32[128,1]{0,1:T(1,128)S(1)}, s32[128,1]{0,1:T(1,128)}, u32[]{:S(2)}) copy-start(s32[128,1]{0,1:T(1,128)} %param.21) | copy-start | bytes 1540
  275.0 28.8 %all-to-all-start.1 = ((bf16[16,2,16384]{2,1,0:T(2,128)(2,1)}), bf16[16,2,16384]{2,1,0:T(2,128)(2,1)}, u32[]{:S(2)}, u32[]{:S(2)}) async-start(bf16[16,2,16384]{2,1,0:T(2,128)(2,1)} %reshape.112), calls=%async_computation.3 | async-start | bytes 2097152 | tf_op jit(solution)/shard_map/all_to_all | solution.py:110
  314.0 72.5 %copy-start.1 = (bf16[512,2048]{1,0:T(8,128)(2,1)S(1)}, bf16[512,2048]{1,0:T(8,128)(2,1)}, u32[]{:S(2)}) copy-start(bf16[512,2048]{1,0:T(8,128)(2,1)} %param.15) | copy-start | bytes 6291460
Sparse Core Ops, SparseCore 0:
  9.5 43.8 all-gather.1
  65.4 78.7 reduce-scatter.2
  158.4 78.5 reduce-scatter.4
where the time goes:
time: 395 us; the launch traced here: 393 us
  blocking collectives  139 us (35%)
  other arithmetic  98 us (25%)
  waiting for transfers between devices  57.8 us (15%)
  local copies, waits for them, and re-layouts  50.6 us (13%)
  matrix products  24.3 us (6%)
  between operations  13.3 us (3%)
  starting transfers between devices  9.76 us (2%)
    unnamed x2, other arithmetic  90.5 us
    psum x1, blocking collectives, body(): fresh_sum = lax.psum(kv_part, 'tensor')  76.3 us
    psum x1, blocking collectives, body(): output_factor_rows = lax.psum(factor_part, 'tensor').astype(jnp.bfloat16)  62.9 us
    unnamed x23, local copies, waits for them, and re-layouts  46.5 us
    all_gather x1, waiting for transfers between devices, body(): whole = lax.all_gather(hidden_in, 'tensor', axis=1, tiled=True)  44.7 us
    all_to_all x1, waiting for transfers between devices, body(): lax.all_to_all(output_up_factor, 'tensor', split_axis=2, concat_axis=0, t...  11.9 us
  transfers between devices with their start and end apart: 5, of which 3 were waited for; matrix products, arithmetic and copies ran while one was open for 36% of the time, Pallas kernels for 0%

commit v1 on v0

v1 whole, which is shorter than its diff:
```python
import functools

import jax
import jax.numpy as jnp
from jax import lax
from jax.experimental import pallas as pl
from jax.experimental.pallas import tpu as pltpu
from jax.sharding import PartitionSpec as P

H = 64
KVH = 8
HD = 128
MESH = pl.DeviceIdType.MESH
F32 = jnp.float32
BF16 = jnp.bfloat16

adapter_scale = 2.0


def chip_of(p, chips):
    if chips == 8:
        return 2 * p + lax.div(p, 4) * (15 - 4 * p)
    return p


def place_of(c, chips):
    if chips == 8:
        z = lax.div(c, 2)
        return z + lax.rem(c, 2) * (7 - 2 * z)
    return c


class Ring:
    def __init__(self, n):
        self.n = n
        self.chips = n // 2
        self.long = self.chips // 2
        self.short = self.chips - 1 - self.long
        self.me = lax.axis_index("tensor")
        self.core = lax.rem(self.me, 2)
        self.place = place_of(lax.div(self.me, 2), self.chips)
        self.sign = 1 - 2 * self.core
        self.right = self.at(1)
        self.left = self.at(-1)
        self.mate = self.chip(0) * 2 + 1 - self.core

    def chip(self, off):
        return chip_of(
            lax.rem(self.place + off * self.sign + 2 * self.chips, self.chips), self.chips
        )

    def at(self, off, other=False):
        core = 1 - self.core if other else self.core
        return self.chip(off) * 2 + core

    def barrier(self):
        sem = pltpu.get_barrier_semaphore()
        for device in (self.right, self.left, self.mate):
            pl.semaphore_signal(sem, inc=1, device_id={"tensor": device}, device_id_type=MESH)
        pl.semaphore_wait(sem, 3)

    def copy(self, src, dst, ssem, rsem, device):
        return pltpu.make_async_remote_copy(
            src_ref=src,
            dst_ref=dst,
            send_sem=ssem,
            recv_sem=rsem,
            device_id={"tensor": device},
            device_id_type=MESH,
        )


def gather_sems(n):
    return [pltpu.SemaphoreType.DMA((n - 1,)), pltpu.SemaphoreType.DMA((n - 1,))]


def gather_blocks(ring, blocks, ssem, rsem, between, on_block):
    long, short, chips = ring.long, ring.short, ring.chips
    sent = []

    def send(slot, index, device):
        one = ring.copy(blocks.at[slot], blocks.at[slot], ssem.at[index], rsem.at[index], device)
        one.start()
        sent.append(one)

    def arrived(slot, index):
        ring.copy(
            blocks.at[slot], blocks.at[slot], ssem.at[index], rsem.at[index], ring.mate
        ).wait_recv()

    hand = chips - 1
    send(ring.me, 0, ring.right)
    send(ring.me, long, ring.left)
    send(ring.me, hand, ring.mate)
    between()
    arrived(ring.mate, hand)
    on_block(ring.mate)
    for j in range(1, long + 1):
        slot = ring.at(-j)
        arrived(slot, j - 1)
        if j < long:
            send(slot, j, ring.right)
        send(slot, hand + j, ring.mate)
        if j <= short:
            other = ring.at(j)
            arrived(other, long + j - 1)
            if j < short:
                send(other, long + j, ring.left)
            send(other, hand + long + j, ring.mate)
        on_block(slot)
        if j <= short:
            on_block(other)
        slot = ring.at(j, True)
        arrived(slot, hand + j)
        on_block(slot)
        if j <= short:
            slot = ring.at(-j, True)
            arrived(slot, hand + long + j)
            on_block(slot)
    for one in sent:
        one.wait_send()


def scatter_scratch(n, rows, width):
    chips = n // 2
    return [
        pltpu.VMEM((chips, rows, width), BF16),
        pltpu.VMEM((chips, rows, width), BF16),
        pltpu.VMEM((chips - 1, rows, width), BF16),
        pltpu.VMEM((chips - 1, rows, width), BF16),
        pltpu.SemaphoreType.DMA((n - 1,)),
        pltpu.SemaphoreType.DMA((n - 1,)),
    ]


def scatter_sum(ring, partial, hand_out, hand_in, going, coming, ssem, rsem):
    long, short, chips = ring.long, ring.short, ring.chips
    order = []
    for j in range(long, 0, -1):
        order.append(j)
        if j > 1:
            order.append(1 - j)
    order = [o for o in order if -short <= o <= long] + [0]
    sent = []
    base = chips - 1
    for i, o in enumerate(order):
        hand_out[i] = partial(ring.chip(-o), 1 - ring.core).astype(BF16)
        one = ring.copy(
            hand_out.at[i], hand_in.at[i], ssem.at[base + i], rsem.at[base + i], ring.mate
        )
        one.start()
        sent.append(one)

    def arrived(buf, index, sem):
        ring.copy(buf.at[index], buf.at[index], ssem.at[sem], rsem.at[sem], ring.mate).wait_recv()
        return buf[index].astype(F32)

    for i, o in enumerate(order):
        value = partial(ring.chip(o), ring.core)
        value = value + arrived(hand_in, i, base + i)
        if o > 0:
            step = long - o
            first, device, slot = step == 0, ring.right, step
        elif o < 0:
            step = short + o
            first, device, slot = step == 0, ring.left, long + step
        else:
            value = value + arrived(coming, long - 1, long - 1)
            if short:
                value = value + arrived(coming, long + short - 1, long + short - 1)
            break
        if not first:
            value = value + arrived(coming, slot - 1, slot - 1)
        going[slot] = value.astype(BF16)
        one = ring.copy(going.at[slot], coming.at[slot], ssem.at[slot], rsem.at[slot], device)
        one.start()
        sent.append(one)
    for one in sent:
        one.wait_send()
    return value


def columns(index, width):
    return pl.ds(pl.multiple_of(index * width, width), width)


def dot(a, b):
    return jnp.dot(a, b, preferred_element_type=F32)


def dot_t(a, b):
    return lax.dot_general(a, b, (((1,), (1,)), ((), ())), preferred_element_type=F32)


def first_kernel(
    n,
    hidden,
    gain,
    ids,
    wq_hbm,
    kvw_hbm,
    down_hbm,
    up_hbm,
    query,
    pair,
    blocks,
    wq,
    kvw,
    down,
    up,
    normed,
    total,
    factor,
    halves,
    wsem,
    gs,
    gr,
    fsem,
    *scatter,
):
    ring = Ring(n)
    loads = [
        pltpu.make_async_copy(src, dst, wsem.at[i])
        for i, (src, dst) in enumerate(
            ((wq_hbm, wq), (down_hbm, down), (kvw_hbm, kvw), (up_hbm, up))
        )
    ]
    for load in loads:
        load.start()
    rows, width = hidden.shape
    blocks[ring.me] = hidden[...]
    ring.barrier()

    def add_square(x):
        wide = x.astype(F32)
        total[...] += jnp.sum(wide * wide, axis=1, keepdims=True)

    def between():
        total[...] = jnp.zeros_like(total)
        add_square(hidden[...])
        query_sum[...] = jnp.zeros_like(query_sum)
        factor[...] = jnp.zeros_like(factor)

    query_sum = scatter[-1]
    scatter = scatter[:-1]
    gather_blocks(ring, blocks, gs, gr, between, lambda slot: add_square(blocks[slot]))
    inverse = lax.rsqrt(total[...] * (1.0 / (n * width)) + 1e-06)
    for load in loads:
        load.wait()

    def project(t, carry):
        part = columns(t, width)
        x = (blocks[t].astype(F32) * inverse * gain[:, part].astype(F32)).astype(BF16)
        normed[t] = x
        query_sum[...] += dot(x, wq[part, :])
        factor[...] += dot_t(x, down[:, part])
        return carry

    lax.fori_loop(0, n, project, 0)
    masked = jnp.where(ids[...] == ring.me, factor[...], 0.0).astype(BF16)
    own = normed[ring.me]
    devices_a_head = n // KVH

    def partial(chip, core):
        head = lax.div(chip * 2, devices_a_head)
        delta = dot(masked, up[:, columns(chip * 2 + core, width)])
        fresh = dot(own, kvw[:, columns(head * 2 + core, HD)])
        return jnp.concatenate([delta, fresh], axis=1)

    value = scatter_sum(ring, partial, *scatter)
    halves[ring.core] = value[:, width:].astype(BF16)
    swap = ring.copy(
        halves.at[ring.core], halves.at[ring.core], fsem.at[0], fsem.at[1], ring.mate
    )
    swap.start()
    query[...] = (query_sum[...] + adapter_scale * value[:, :width]).astype(BF16)
    swap.wait_send()
    other = halves.at[1 - ring.core]
    ring.copy(other, other, fsem.at[0], fsem.at[1], ring.mate).wait_recv()
    pair[...] = halves[...]


def second_kernel(
    n,
    attended,
    ids,
    wo_hbm,
    down_hbm,
    up_hbm,
    out,
    blocks,
    wo,
    down,
    up,
    base,
    factor,
    wsem,
    gs,
    gr,
    *scatter,
):
    ring = Ring(n)
    loads = [
        pltpu.make_async_copy(src, dst, wsem.at[i])
        for i, (src, dst) in enumerate(((wo_hbm, wo), (down_hbm, down), (up_hbm, up)))
    ]
    for load in loads:
        load.start()
    rows, width = attended.shape
    blocks[ring.me] = attended[...]
    ring.barrier()

    def on_block(slot):
        factor[...] += dot_t(blocks[slot], down[:, columns(slot, width)])

    def between():
        for load in loads:
            load.wait()

        def one(t, carry):
            base[t] = dot(attended[...], wo[:, columns(t, width)])
            return carry

        lax.fori_loop(0, n, one, 0)
        factor[...] = dot_t(attended[...], down[:, columns(ring.me, width)])

    gather_blocks(ring, blocks, gs, gr, between, on_block)
    masked = jnp.where(ids[...] == ring.me, factor[...], 0.0).astype(BF16)

    def partial(chip, core):
        t = chip * 2 + core
        return base[t] + adapter_scale * dot(masked, up[:, columns(t, width)])

    out[...] = scatter_sum(ring, partial, *scatter).astype(BF16)


VM = pl.BlockSpec(memory_space=pltpu.VMEM)
ANY = pl.BlockSpec(memory_space=pl.ANY)


def body(
    hidden_in,
    norm_gain,
    query_base_matrix,
    kv_weight,
    out_weight,
    query_down,
    query_up_factor,
    output_down,
    output_up_factor,
    variant_ids,
    cache_lengths,
    kv_cache,
):
    n = lax.axis_size("tensor")
    rows, width = hidden_in.shape
    depth = norm_gain.shape[0]
    rank = query_down.shape[2]
    params = functools.partial(
        pltpu.CompilerParams, has_side_effects=True, vmem_limit_bytes=48 * 1024 * 1024
    )
    query_vectors, pair = pl.pallas_call(
        functools.partial(first_kernel, n),
        out_shape=[
            jax.ShapeDtypeStruct((rows, width), BF16),
            jax.ShapeDtypeStruct((2, rows, HD), BF16),
        ],
        in_specs=[VM] * 3 + [ANY] * 4,
        out_specs=[VM] * 2,
        scratch_shapes=[
            pltpu.VMEM((n, rows, width), BF16),
            pltpu.VMEM(query_base_matrix.shape, BF16),
            pltpu.VMEM(kv_weight.shape, BF16),
            pltpu.VMEM((rank, depth), BF16),
            pltpu.VMEM((rank, depth), BF16),
            pltpu.VMEM((n, rows, width), BF16),
            pltpu.VMEM((rows, 1), F32),
            pltpu.VMEM((rows, rank), F32),
            pltpu.VMEM((2, rows, HD), BF16),
            pltpu.SemaphoreType.DMA((4,)),
            *gather_sems(n),
            pltpu.SemaphoreType.DMA((2,)),
            *scatter_scratch(n, rows, width + HD),
            pltpu.VMEM((rows, width), F32),
        ],
        compiler_params=params(collective_id=0),
        name="gather_project",
    )(
        hidden_in,
        norm_gain[None],
        variant_ids,
        query_base_matrix,
        kv_weight,
        jnp.swapaxes(query_down, 1, 2)[0],
        query_up_factor[0],
    )
    fresh_key, fresh_value = pair[0], pair[1]
    local_heads = width // HD
    query_heads = query_vectors.reshape(rows, local_heads, HD)
    stored = kv_cache[0]
    keys = stored[:, :, :HD]
    values = stored[:, :, HD:]
    scale = 1.0 / HD**0.5
    scores = (
        jnp.einsum("rhd,rld->rhl", query_heads, keys, preferred_element_type=F32) * scale
    )
    own = jnp.einsum("rhd,rd->rh", query_heads, fresh_key, preferred_element_type=F32) * scale
    positions = jnp.arange(stored.shape[1], dtype=jnp.int32)
    live = positions[None, :] < cache_lengths[:, None]
    scores = jnp.where(live[:, None, :], scores, -jnp.inf)
    top = jnp.maximum(jnp.max(scores, axis=2), own)
    expo = jnp.exp(scores - top[:, :, None])
    own_expo = jnp.exp(own - top)
    total = jnp.sum(expo, axis=2) + own_expo
    weights = (expo / total[:, :, None]).astype(BF16)
    own_weight = (own_expo / total).astype(BF16)
    mixed_heads = jnp.einsum("rhl,rld->rhd", weights, values, preferred_element_type=F32)
    mixed_heads = (
        mixed_heads + own_weight.astype(F32)[:, :, None] * fresh_value.astype(F32)[:, None, :]
    )
    attended = mixed_heads.astype(BF16).reshape(rows, local_heads * HD)
    return pl.pallas_call(
        functools.partial(second_kernel, n),
        out_shape=jax.ShapeDtypeStruct((rows, width), BF16),
        in_specs=[VM] * 2 + [ANY] * 3,
        out_specs=VM,
        scratch_shapes=[
            pltpu.VMEM((n, rows, width), BF16),
            pltpu.VMEM(out_weight.shape, BF16),
            pltpu.VMEM((rank, depth), BF16),
            pltpu.VMEM((rank, depth), BF16),
            pltpu.VMEM((n, rows, width), F32),
            pltpu.VMEM((rows, rank), F32),
            pltpu.SemaphoreType.DMA((3,)),
            *gather_sems(n),
            *scatter_scratch(n, rows, width),
        ],
        compiler_params=params(collective_id=1),
        name="gather_output",
    )(
        attended,
        variant_ids,
        out_weight,
        jnp.swapaxes(output_down, 1, 2)[0],
        output_up_factor[0],
    )


def solution(mesh):
    in_specs = (
        P("groups", "tensor"),
        P(),
        P(None, "tensor"),
        P("tensor", None),
        P("tensor", None),
        P("tensor", None, None),
        P("tensor", None, None),
        P("tensor", None, None),
        P("tensor", None, None),
        P("groups", None),
        P("groups"),
        P("tensor", "groups", None, None),
    )
    out_specs = P("groups", "tensor")
    return jax.shard_map(body, mesh=mesh, in_specs=in_specs, out_specs=out_specs, check_vma=False)
```

time: 395 us -> 107 us (0.27)
  blocking collectives: 139 us -> 0 us
  other arithmetic: 98 us -> 1.16 us
  Pallas kernels: 0 us -> 94.4 us
  waiting for transfers between devices: 57.8 us -> 0 us
  local copies, waits for them, and re-layouts: 50.6 us -> 7.7 us
  matrix products: 24.3 us -> 3.35 us
  between operations: 13.3 us -> 0.12 us
  starting transfers between devices: 9.76 us -> 0 us
    psum x2 -> x0, blocking collectives: 139 us -> none  [the longest x1 76.3 us: body(): fresh_sum = lax.psum(kv_part, 'tensor')]
    pallas_call x0 -> x2, Pallas kernels: none -> 94.4 us  [the longest x1 51.9 us: body(): pl.pallas_call(functools.partial(first_kernel, n), out_shape=[jax.ShapeDt...]
    unnamed x2 -> x0, other arithmetic: 90.5 us -> none
    all_gather x1 -> x0, waiting for transfers between devices: 44.7 us -> none  [body(): whole = lax.all_gather(hidden_in, 'tensor', axis=1, tiled=True)]
    unnamed x23 -> x15, local copies, waits for them, and re-layouts: 46.5 us -> 6.39 us
    dot_general x8 -> x3, matrix products: 22.6 us -> 3.35 us  [the longest x1 1.54 us: body(): jnp.einsum('rhd,rld->rhl', query_heads, keys, preferred_element_type=F32)]
    all_to_all x2 -> x0, waiting for transfers between devices: 11.9 us -> none  [the longest x1 11.9 us: body(): lax.all_to_all(output_up_factor, 'tensor', split_axis=2, concat_axis=0, t...]
    all_to_all x2 -> x0, starting transfers between devices: 9.68 us -> none  [the longest x1 5.8 us: body(): lax.all_to_all(output_up_factor, 'tensor', split_axis=2, concat_axis=0, t...]
  transfers between devices with their start and end apart: 5 -> 0, of which waited for: 3 -> 0; matrix products, arithmetic and copies ran while one was open for 36% -> 0% of each run, Pallas kernels for 0% -> 0%
where the time goes in v1:
time: 107 us
  Pallas kernels  94.4 us (88%)
  local copies, waits for them, and re-layouts  7.7 us (7%)
  matrix products  3.35 us (3%)
  other arithmetic  1.16 us (1%)
    pallas_call x1, Pallas kernels, body(): pl.pallas_call(functools.partial(first_kernel, n), out_shape=[jax.ShapeDt...  51.9 us
    pallas_call x1, Pallas kernels, body(): pl.pallas_call(functools.partial(second_kernel, n), out_shape=jax.ShapeDt...  42.5 us
    unnamed x15, local copies, waits for them, and re-layouts  6.39 us

profile of v1, /device:TPU:0, one launch (start us, length us, event | category | flops | bytes accessed | tf_op | source)
XLA Modules:
  0.0 106.7 jit_solution(9185778023187099198)
XLA Ops:
  0.0 0.7 iota_compare_fusion
  0.7 0.7 broadcast_in_dim.15.gain
  1.5 0.8 copy.20.ids
  2.2 0.0 copy-start
  2.3 1.6 %copy-done = bf16[512,2048]{1,0:T(8,128)(2,1)S(1)} copy-done((bf16[512,2048]{1,0:T(8,128)(2,1)S(1)}, bf16[512,2048]{1,0:T(8,128)(2,1)}, u32[]{:S(2)}) %copy-start) | copy-done | bytes 2097176
  3.8 0.0 copy-start.1
  3.8 1.2 %copy-done.1 = bf16[1,8192,64]{1,2,0:T(8,128)(2,1)S(1)} copy-done((bf16[1,8192,64]{1,2,0:T(8,128)(2,1)S(1)}, bf16[1,8192,64]{1,2,0:T(8,128)(2,1)}, u32[]{:S(2)}) %copy-start.1) | copy-done | bytes 1048600
  5.1 0.0 copy-start.2
  5.1 1.2 %copy-done.2 = bf16[1,64,8192]{2,1,0:T(8,128)(2,1)S(1)} copy-done((bf16[1,64,8192]{2,1,0:T(8,128)(2,1)S(1)}, bf16[1,64,8192]{2,1,0:T(8,128)(2,1)}, u32[]{:S(2)}) %copy-start.2) | copy-done | bytes 1048600
  6.3 0.0 copy-start.5
  6.3 0.9 copy-done.5
  7.2 0.0 copy-start.3
  7.2 0.0 copy-start.4
  7.2 51.9 %gather_project.1 = (bf16[128,512]{1,0:T(8,128)(2,1)S(1)}, bf16[2,128,128]{2,1,0:T(8,128)(2,1)S(1)}) custom-call(bf16[128,512]{1,0:T(8,128)(2,1)S(1)} %copy-done.5, bf16[1,8192]{1,0:T(2,128)(2,1)S(1)} %broadcast_in_dim.15.gain, s32[128,1]{1,0:T(8,128)S(1)} %copy.20.ids, bf16[8192,512]{1,0:T(8,128)(2,1)} %wq_hbm.1, bf16[512,2048]{1,0:T(8,128)(2,1)S(1)} %copy-done, ...), custom_call_target="tpu_custom_call" | custom-call | tf_op jit(solution)/shard_map/gather_project/pallas_call | solution.py:362
  59.2 0.3 fusion.7
  59.4 0.1 copy.28
  59.5 1.5 %fusion.12 = (f32[128,4]{1,0:T(8,128)S(1)}, f32[128,4,16]{2,1,0:T(4,128)S(1)}) fusion(bf16[128,4,128]{2,1,0:T(4,128)(2,1)S(1)} %reshape.33, bf16[128,16,256]{2,1,0:T(8,128)(2,1)} %bitcast.43, pred[128,16]{1,0:T(8,128)(4,1)S(1)} %iota_compare_fusion), kind=kOutput, calls=%fused_computation.23 | convolution fusion | flops 2121216 | bytes 692224 | tf_op jit(solution)/shard_map/rhd,rld->rhl/dot_general | solution.py:405
  61.0 0.1 copy.21
  61.1 0.1 copy.22
  61.2 0.4 fusion.4
  61.6 0.1 copy.23
  61.7 0.1 copy.24
  61.9 0.1 copy.25
  62.0 1.5 %fusion.1 = bf16[128,4,128]{2,1,0:T(4,128)(2,1)S(1)} fusion(bf16[128,16,256]{2,1,0:T(8,128)(2,1)} %bitcast.44, f32[128,4,16]{2,1,0:T(4,128)S(1)} %get-tuple-element.14, f32[128,128]{1,0:T(8,128)S(1)} %get-tuple-element.10, f32[128,4]{1,0:T(8,128)S(1)} %copy.25, f32[128,4]{1,0:T(8,128)S(1)} %copy.24, f32[128,4]{1,0:T(8,128)S(1)} %copy.22), kind=kOutput, calls=%fused_computation.3 | convolution fusion | flops 2318336 | bytes 759808 | tf_op jit(solution)/shard_map/rhl,rld->rhd/dot_general | solution.py:417
  63.5 0.0 copy-done.3
  63.5 0.0 copy-done.4
  63.6 42.5 %gather_output.1 = bf16[128,512]{1,0:T(8,128)(2,1)S(1)} custom-call(bf16[128,512]{1,0:T(8,128)(2,1)S(1)} %bitcast.41, s32[128,1]{1,0:T(8,128)S(1)} %copy.20.ids, bf16[512,8192]{1,0:T(8,128)(2,1)} %wo_hbm.1, bf16[64,8192]{1,0:T(8,128)(2,1)S(1)} %bitcast.39, bf16[64,8192]{1,0:T(8,128)(2,1)S(1)} %bitcast.40), custom_call_target="tpu_custom_call" | custom-call | tf_op jit(solution)/shard_map/gather_output/pallas_call | solution.py:422
  106.1 0.7 copy.35
  (5 shorter events, 0.1 us)
Async XLA Ops:
  2.2 1.6 %copy-start = (bf16[512,2048]{1,0:T(8,128)(2,1)S(1)}, bf16[512,2048]{1,0:T(8,128)(2,1)}, u32[]{:S(2)}) copy-start(bf16[512,2048]{1,0:T(8,128)(2,1)} %kvw_hbm.1) | copy-start | bytes 6291460
  3.8 1.2 %copy-start.1 = (bf16[1,8192,64]{1,2,0:T(8,128)(2,1)S(1)}, bf16[1,8192,64]{1,2,0:T(8,128)(2,1)}, u32[]{:S(2)}) copy-start(bf16[1,8192,64]{1,2,0:T(8,128)(2,1)} %param.17) | copy-start | bytes 3145732
  5.1 1.2 %copy-start.2 = (bf16[1,64,8192]{2,1,0:T(8,128)(2,1)S(1)}, bf16[1,64,8192]{2,1,0:T(8,128)(2,1)}, u32[]{:S(2)}) copy-start(bf16[1,64,8192]{2,1,0:T(8,128)(2,1)} %param.18) | copy-start | bytes 3145732
  6.3 0.9 copy-start.5
  7.2 56.3 %copy-start.3 = (bf16[1,8192,64]{1,2,0:T(8,128)(2,1)S(1)}, bf16[1,8192,64]{1,2,0:T(8,128)(2,1)}, u32[]{:S(2)}) copy-start(bf16[1,8192,64]{1,2,0:T(8,128)(2,1)} %param.19) | copy-start | bytes 3145732
  7.2 56.3 %copy-start.4 = (bf16[1,64,8192]{2,1,0:T(8,128)(2,1)S(1)}, bf16[1,64,8192]{2,1,0:T(8,128)(2,1)}, u32[]{:S(2)}) copy-start(bf16[1,64,8192]{2,1,0:T(8,128)(2,1)} %param.20) | copy-start | bytes 3145732

commit v2 on v1

--- a/solution.py
+++ b/solution.py
@@ -13,6 +13,7 @@
 MESH = pl.DeviceIdType.MESH
 F32 = jnp.float32
 BF16 = jnp.bfloat16
+VMEM_LIMIT = 62 * 1024 * 1024
 
 adapter_scale = 2.0
 
@@ -71,52 +72,62 @@
 
 
 def gather_sems(n):
-    return [pltpu.SemaphoreType.DMA((n - 1,)), pltpu.SemaphoreType.DMA((n - 1,))]
-
-
-def gather_blocks(ring, blocks, ssem, rsem, between, on_block):
+    return [pltpu.SemaphoreType.DMA((2, n - 1)), pltpu.SemaphoreType.DMA((2, n - 1))]
+
+
+def half(ref, slot, h):
+    rows = ref.shape[1] // 2
+    return ref.at[slot, pl.ds(h * rows, rows)]
+
+
+def gather_blocks(ring, blocks, ssem, rsem, filler, on_block):
     long, short, chips = ring.long, ring.short, ring.chips
     sent = []
 
-    def send(slot, index, device):
-        one = ring.copy(blocks.at[slot], blocks.at[slot], ssem.at[index], rsem.at[index], device)
+    def copy(slot, h, index, device):
+        ref = half(blocks, slot, h)
+        return ring.copy(ref, ref, ssem.at[h, index], rsem.at[h, index], device)
+
+    def send(slot, h, index, device):
+        one = copy(slot, h, index, device)
         one.start()
         sent.append(one)
 
-    def arrived(slot, index):
-        ring.copy(
-            blocks.at[slot], blocks.at[slot], ssem.at[index], rsem.at[index], ring.mate
-        ).wait_recv()
-
     hand = chips - 1
-    send(ring.me, 0, ring.right)
-    send(ring.me, long, ring.left)
-    send(ring.me, hand, ring.mate)
-    between()
-    arrived(ring.mate, hand)
-    on_block(ring.mate)
+    for h in range(2):
+        send(ring.me, h, 0, ring.right)
+        send(ring.me, h, long, ring.left)
+    for h in range(2):
+        send(ring.me, h, hand, ring.mate)
+    filler(0)
+    waiting = [(ring.mate, hand)]
+    ready = []
     for j in range(1, long + 1):
-        slot = ring.at(-j)
-        arrived(slot, j - 1)
-        if j < long:
-            send(slot, j, ring.right)
-        send(slot, hand + j, ring.mate)
-        if j <= short:
-            other = ring.at(j)
-            arrived(other, long + j - 1)
-            if j < short:
-                send(other, long + j, ring.left)
-            send(other, hand + long + j, ring.mate)
+        slot, other = ring.at(-j), ring.at(j)
+        for h in range(2):
+            copy(slot, h, j - 1, ring.mate).wait_recv()
+            if j < long:
+                send(slot, h, j, ring.right)
+            send(slot, h, hand + j, ring.mate)
+            if j <= short:
+                copy(other, h, long + j - 1, ring.mate).wait_recv()
+                if j < short:
+                    send(other, h, long + j, ring.left)
+                send(other, h, hand + long + j, ring.mate)
+        filler(j)
+        for done, index in waiting:
+            for h in range(2):
+                copy(done, h, index, ring.mate).wait_recv()
+            on_block(done)
         on_block(slot)
+        waiting = [(ring.at(j, True), hand + j)]
         if j <= short:
             on_block(other)
-        slot = ring.at(j, True)
-        arrived(slot, hand + j)
-        on_block(slot)
-        if j <= short:
-            slot = ring.at(-j, True)
-            arrived(slot, hand + long + j)
-            on_block(slot)
+            waiting.append((ring.at(-j, True), hand + long + j))
+    for done, index in waiting:
+        for h in range(2):
+            copy(done, h, index, ring.mate).wait_recv()
+        on_block(done)
     for one in sent:
         one.wait_send()
 
@@ -128,56 +139,92 @@
         pltpu.VMEM((chips, rows, width), BF16),
         pltpu.VMEM((chips - 1, rows, width), BF16),
         pltpu.VMEM((chips - 1, rows, width), BF16),
-        pltpu.SemaphoreType.DMA((n - 1,)),
-        pltpu.SemaphoreType.DMA((n - 1,)),
+        pltpu.VMEM((2, rows, width), F32),
+        pltpu.SemaphoreType.DMA((chips,)),
+        pltpu.SemaphoreType.DMA((chips,)),
+        pltpu.SemaphoreType.DMA((2, chips - 1)),
+        pltpu.SemaphoreType.DMA((2, chips - 1)),
     ]
 
 
-def scatter_sum(ring, partial, hand_out, hand_in, going, coming, ssem, rsem):
+def scatter_sum(ring, partial, filler, hand_out, hand_in, going, coming, held, hs, hr, ssem, rsem):
     long, short, chips = ring.long, ring.short, ring.chips
-    order = []
-    for j in range(long, 0, -1):
-        order.append(j)
-        if j > 1:
-            order.append(1 - j)
-    order = [o for o in order if -short <= o <= long] + [0]
+    rows = going.shape[1] // 2
+    steps = []
+    for j in range(1, long + 1):
+        now = [(2 * j - 2, long - j + 1, j - 1, ring.right, j == 1)]
+        if j <= short:
+            now.append((2 * j - 1, j - short - 1, long + j - 1, ring.left, j == 1))
+        steps.append(now)
     sent = []
-    base = chips - 1
-    for i, o in enumerate(order):
-        hand_out[i] = partial(ring.chip(-o), 1 - ring.core).astype(BF16)
-        one = ring.copy(
-            hand_out.at[i], hand_in.at[i], ssem.at[base + i], rsem.at[base + i], ring.mate
-        )
+
+    def start(one):
         one.start()
         sent.append(one)
 
-    def arrived(buf, index, sem):
-        ring.copy(buf.at[index], buf.at[index], ssem.at[sem], rsem.at[sem], ring.mate).wait_recv()
-        return buf[index].astype(F32)
-
-    for i, o in enumerate(order):
+    def hand_copy(i):
+        return ring.copy(hand_out.at[i], hand_in.at[i], hs.at[i], hr.at[i], ring.mate)
+
+    def hand_over(i, o):
+        hand_out[i] = partial(ring.chip(-o), 1 - ring.core).astype(BF16)
+        start(hand_copy(i))
+
+    def hand_overs(j):
+        if j < long:
+            for i, o, _, _, _ in steps[j]:
+                hand_over(i, o)
+        elif j == long:
+            hand_over(chips - 1, 0)
+
+    def both(i, o):
         value = partial(ring.chip(o), ring.core)
-        value = value + arrived(hand_in, i, base + i)
-        if o > 0:
-            step = long - o
-            first, device, slot = step == 0, ring.right, step
-        elif o < 0:
-            step = short + o
-            first, device, slot = step == 0, ring.left, long + step
-        else:
-            value = value + arrived(coming, long - 1, long - 1)
-            if short:
-                value = value + arrived(coming, long + short - 1, long + short - 1)
-            break
-        if not first:
-            value = value + arrived(coming, slot - 1, slot - 1)
-        going[slot] = value.astype(BF16)
-        one = ring.copy(going.at[slot], coming.at[slot], ssem.at[slot], rsem.at[slot], device)
-        one.start()
-        sent.append(one)
+        ring.copy(hand_in.at[i], hand_in.at[i], hs.at[i], hr.at[i], ring.mate).wait_recv()
+        return value + hand_in[i].astype(F32)
+
+    def arrived(slot, h):
+        ref = half(coming, slot, h)
+        ring.copy(ref, ref, ssem.at[h, slot], rsem.at[h, slot], ring.mate).wait_recv()
+        return ref[...].astype(F32)
+
+    hand_overs(0)
+    hand_overs(1)
+    for j, now in enumerate(steps):
+        for place, (i, o, slot, device, first) in enumerate(now):
+            held[place] = both(i, o)
+        for h in range(2):
+            part = pl.ds(h * rows, rows)
+            for place, (i, o, slot, device, first) in enumerate(now):
+                value = held[place, part]
+                if not first:
+                    value = value + arrived(slot - 1, h)
+                going[slot, part] = value.astype(BF16)
+                start(
+                    ring.copy(
+                        half(going, slot, h),
+                        half(coming, slot, h),
+                        ssem.at[h, slot],
+                        rsem.at[h, slot],
+                        device,
+                    )
+                )
+        hand_overs(j + 2)
+        filler(j)
+    if long < 2:
+        hand_overs(long)
+    held[0] = both(chips - 1, 0)
+    for h in range(2):
+        part = pl.ds(h * rows, rows)
+        value = held[0, part] + arrived(long - 1, h)
+        if short:
+            value = value + arrived(long + short - 1, h)
+        held[0, part] = value
     for one in sent:
         one.wait_send()
-    return value
+    return held[0]
+
+
+def share(step, steps, count):
+    return range(count * step // steps, count * (step + 1) // steps)
 
 
 def columns(index, width):
@@ -235,29 +282,29 @@
         wide = x.astype(F32)
         total[...] += jnp.sum(wide * wide, axis=1, keepdims=True)
 
-    def between():
-        total[...] = jnp.zeros_like(total)
-        add_square(hidden[...])
-        query_sum[...] = jnp.zeros_like(query_sum)
-        factor[...] = jnp.zeros_like(factor)
+    def prepare(step):
+        if step == 0:
+            total[...] = jnp.zeros_like(total)
+            add_square(hidden[...])
+            query_sum[...] = jnp.zeros_like(query_sum)
+            factor[...] = jnp.zeros_like(factor)
 
     query_sum = scatter[-1]
     scatter = scatter[:-1]
-    gather_blocks(ring, blocks, gs, gr, between, lambda slot: add_square(blocks[slot]))
+    gather_blocks(ring, blocks, gs, gr, prepare, lambda slot: add_square(blocks[slot]))
     inverse = lax.rsqrt(total[...] * (1.0 / (n * width)) + 1e-06)
     for load in loads:
         load.wait()
 
-    def project(t, carry):
+    def normalize(t, carry):
         part = columns(t, width)
         x = (blocks[t].astype(F32) * inverse * gain[:, part].astype(F32)).astype(BF16)
         normed[t] = x
-        query_sum[...] += dot(x, wq[part, :])
-        factor[...] += dot_t(x, down[:, part])
+        factor[...] += dot_t(down[:, part], x)
         return carry
 
-    lax.fori_loop(0, n, project, 0)
-    masked = jnp.where(ids[...] == ring.me, factor[...], 0.0).astype(BF16)
+    lax.fori_loop(0, n, normalize, 0)
+    masked = jnp.where(ids[...] == ring.me, factor[...], 0.0).T.astype(BF16)
     own = normed[ring.me]
     devices_a_head = n // KVH
 
@@ -267,7 +314,15 @@
         fresh = dot(own, kvw[:, columns(head * 2 + core, HD)])
         return jnp.concatenate([delta, fresh], axis=1)
 
-    value = scatter_sum(ring, partial, *scatter)
+    def project(t, carry):
+        query_sum[...] += dot(normed[t], wq[columns(t, width), :])
+        return carry
+
+    def projects(step):
+        part = share(step, ring.long, n)
+        lax.fori_loop(part.start, part.stop, project, 0)
+
+    value = scatter_sum(ring, partial, projects, *scatter)
     halves[ring.core] = value[:, width:].astype(BF16)
     swap = ring.copy(
         halves.at[ring.core], halves.at[ring.core], fsem.at[0], fsem.at[1], ring.mate
@@ -302,7 +357,7 @@
     ring = Ring(n)
     loads = [
         pltpu.make_async_copy(src, dst, wsem.at[i])
-        for i, (src, dst) in enumerate(((wo_hbm, wo), (down_hbm, down), (up_hbm, up)))
+        for i, (src, dst) in enumerate(((down_hbm, down), (wo_hbm, wo), (up_hbm, up)))
     ]
     for load in loads:
         load.start()
@@ -311,27 +366,31 @@
     ring.barrier()
 
     def on_block(slot):
-        factor[...] += dot_t(blocks[slot], down[:, columns(slot, width)])
-
-    def between():
-        for load in loads:
-            load.wait()
-
-        def one(t, carry):
-            base[t] = dot(attended[...], wo[:, columns(t, width)])
-            return carry
-
-        lax.fori_loop(0, n, one, 0)
-        factor[...] = dot_t(attended[...], down[:, columns(ring.me, width)])
-
-    gather_blocks(ring, blocks, gs, gr, between, on_block)
-    masked = jnp.where(ids[...] == ring.me, factor[...], 0.0).astype(BF16)
+        factor[...] += dot_t(down[:, columns(slot, width)], blocks[slot])
+
+    def base_product(t, carry):
+        base[t] = dot(attended[...], wo[:, columns(t, width)])
+        return carry
+
+    def fill(step):
+        if step == 0:
+            loads[0].wait()
+            factor[...] = dot_t(down[:, columns(ring.me, width)], attended[...])
+            return
+        if step == 1:
+            loads[1].wait()
+            loads[2].wait()
+        part = share(step - 1, ring.long, n)
+        lax.fori_loop(part.start, part.stop, base_product, 0)
+
+    gather_blocks(ring, blocks, gs, gr, fill, on_block)
+    masked = jnp.where(ids[...] == ring.me, factor[...], 0.0).T.astype(BF16)
 
     def partial(chip, core):
         t = chip * 2 + core
         return base[t] + adapter_scale * dot(masked, up[:, columns(t, width)])
 
-    out[...] = scatter_sum(ring, partial, *scatter).astype(BF16)
+    out[...] = scatter_sum(ring, partial, lambda step: None, *scatter).astype(BF16)
 
 
 VM = pl.BlockSpec(memory_space=pltpu.VMEM)
@@ -357,7 +416,7 @@
     depth = norm_gain.shape[0]
     rank = query_down.shape[2]
     params = functools.partial(
-        pltpu.CompilerParams, has_side_effects=True, vmem_limit_bytes=48 * 1024 * 1024
+        pltpu.CompilerParams, has_side_effects=True, vmem_limit_bytes=VMEM_LIMIT
     )
     query_vectors, pair = pl.pallas_call(
         functools.partial(first_kernel, n),
@@ -375,7 +434,7 @@
             pltpu.VMEM((rank, depth), BF16),
             pltpu.VMEM((n, rows, width), BF16),
             pltpu.VMEM((rows, 1), F32),
-            pltpu.VMEM((rows, rank), F32),
+            pltpu.VMEM((rank, rows), F32),
             pltpu.VMEM((2, rows, HD), BF16),
             pltpu.SemaphoreType.DMA((4,)),
             *gather_sems(n),
@@ -388,7 +447,7 @@
     )(
         hidden_in,
         norm_gain[None],
-        variant_ids,
+        jnp.swapaxes(variant_ids, 0, 1),
         query_base_matrix,
         kv_weight,
         jnp.swapaxes(query_down, 1, 2)[0],
@@ -430,7 +489,7 @@
             pltpu.VMEM((rank, depth), BF16),
             pltpu.VMEM((rank, depth), BF16),
             pltpu.VMEM((n, rows, width), F32),
-            pltpu.VMEM((rows, rank), F32),
+            pltpu.VMEM((rank, rows), F32),
             pltpu.SemaphoreType.DMA((3,)),
             *gather_sems(n),
             *scatter_scratch(n, rows, width),
@@ -439,7 +498,7 @@
         name="gather_output",
     )(
         attended,
-        variant_ids,
+        jnp.swapaxes(variant_ids, 0, 1),
         out_weight,
         jnp.swapaxes(output_down, 1, 2)[0],
         output_up_factor[0],

time: 107 us -> 92.7 us (0.87)
  Pallas kernels: 94.4 us -> 83.9 us
  local copies, waits for them, and re-layouts: 7.7 us -> 5.07 us
  matrix products: 3.35 us -> 1.24 us
    pallas_call x1, Pallas kernels: 51.9 us -> 46.1 us  [body(): pl.pallas_call(functools.partial(first_kernel, n), out_shape=[jax.ShapeDt...]
    pallas_call x1, Pallas kernels: 42.5 us -> 37.9 us  [body(): pl.pallas_call(functools.partial(second_kernel, n), out_shape=jax.ShapeDt...]
    unnamed x15 -> x4, local copies, waits for them, and re-layouts: 6.39 us -> 2.25 us
where the time goes in v2:
time: 92.7 us; the launch traced here: 92.4 us
  Pallas kernels  83.9 us (91%)
  local copies, waits for them, and re-layouts  5.07 us (5%)
  other arithmetic  2.02 us (2%)
  matrix products  1.24 us (1%)
    pallas_call x1, Pallas kernels, body(): pl.pallas_call(functools.partial(first_kernel, n), out_shape=[jax.ShapeDt...  46.1 us
    pallas_call x1, Pallas kernels, body(): pl.pallas_call(functools.partial(second_kernel, n), out_shape=jax.ShapeDt...  37.9 us
    unnamed x4, local copies, waits for them, and re-layouts  2.25 us

profile of v2, /device:TPU:0, one launch (start us, length us, event | category | flops | bytes accessed | tf_op | source)
XLA Modules:
  0.0 92.4 jit_solution(14393956714512265541)
XLA Ops:
  0.0 0.0 copy-start
  0.0 0.8 iota_compare_fusion
  0.8 1.4 %broadcast_in_dim.15.gain = bf16[1,8192]{1,0:T(2,128)(2,1)} reshape(bf16[8192]{0:T(1024)(128)(2,1)} %param.13) | data formatting | bytes 32768 | tf_op jit(solution)/shard_map/broadcast_in_dim | solution.py:449
  2.2 46.1 %gather_project.1 = (bf16[128,512]{1,0:T(8,128)(2,1)}, bf16[2,128,128]{2,1,0:T(8,128)(2,1)}) custom-call(bf16[128,512]{1,0:T(8,128)(2,1)} %hidden.1, bf16[1,8192]{1,0:T(2,128)(2,1)} %broadcast_in_dim.15.gain, s32[1,128]{1,0:T(1,128)} %bitcast.44, bf16[8192,512]{1,0:T(8,128)(2,1)} %wq_hbm.1, bf16[512,2048]{1,0:T(8,128)(2,1)} %kvw_hbm.1, ...), custom_call_target="tpu_custom_call" | custom-call | tf_op jit(solution)/shard_map/gather_project/pallas_call | solution.py:421
  48.3 0.9 %reshape.33 = bf16[128,4,128]{2,1,0:T(4,128)(2,1)S(1)} reshape(bf16[128,512]{1,0:T(8,128)(2,1)} %get-tuple-element.7) | data formatting | bytes 262144 | tf_op jit(solution)/shard_map/reshape | solution.py:458
  49.2 0.8 slice_bitcast_fusion
  50.0 0.3 fusion.7
  50.3 0.1 copy.22
  50.3 0.0 copy-done
  50.3 0.5 fusion.12
  50.8 0.1 copy.16
  50.9 0.1 copy.17
  51.0 0.4 fusion.4
  51.4 0.1 copy.18
  51.5 0.1 copy.19
  51.6 0.1 copy.20
  51.7 0.5 fusion.1
  52.2 0.7 copy.27
  52.9 37.9 %gather_output.1 = bf16[128,512]{1,0:T(8,128)(2,1)} custom-call(bf16[128,512]{1,0:T(8,128)(2,1)} %bitcast.42, s32[1,128]{1,0:T(1,128)} %bitcast.45, bf16[512,8192]{1,0:T(8,128)(2,1)} %wo_hbm.1, bf16[64,8192]{1,0:T(8,128)(2,1)} %bitcast.40, bf16[64,8192]{1,0:T(8,128)(2,1)} %bitcast.41), custom_call_target="tpu_custom_call" | custom-call | tf_op jit(solution)/shard_map/gather_output/pallas_call | solution.py:481
  90.8 1.6 %copy.29 = bf16[128,512]{1,0:T(8,128)(2,1)} copy(bf16[128,512]{1,0:T(8,128)(2,1)} %gather_output.1) | data formatting | bytes 262144
  (2 shorter events, 0.0 us)
Async XLA Ops:
  0.0 50.3 %copy-start = (bf16[1,128,16,256]{3,2,1,0:T(8,128)(2,1)S(1)}, bf16[1,128,16,256]{3,2,1,0:T(8,128)(2,1)}, u32[]{:S(2)}) copy-start(bf16[1,128,16,256]{3,2,1,0:T(8,128)(2,1)} %param.23) | copy-start | bytes 3145732

commit v3 on v2

--- a/solution.py
+++ b/solution.py
@@ -100,6 +100,13 @@
     for h in range(2):
         send(ring.me, h, hand, ring.mate)
     filler(0)
+
+    def mates():
+        for slot, index in waiting:
+            for h in range(2):
+                copy(slot, h, index, ring.mate).wait_recv()
+            on_block(slot)
+
     waiting = [(ring.mate, hand)]
     ready = []
     for j in range(1, long + 1):
@@ -114,20 +121,21 @@
                 if j < short:
                     send(other, h, long + j, ring.left)
                 send(other, h, hand + long + j, ring.mate)
-        filler(j)
-        for done, index in waiting:
-            for h in range(2):
-                copy(done, h, index, ring.mate).wait_recv()
-            on_block(done)
-        on_block(slot)
+            if h == 0:
+                filler(2 * j - 1)
+                for done in ready:
+                    on_block(done)
+            else:
+                mates()
+                filler(2 * j)
+        ready = [slot]
         waiting = [(ring.at(j, True), hand + j)]
         if j <= short:
-            on_block(other)
+            ready.append(other)
             waiting.append((ring.at(-j, True), hand + long + j))
-    for done, index in waiting:
-        for h in range(2):
-            copy(done, h, index, ring.mate).wait_recv()
+    for done in ready:
         on_block(done)
+    mates()
     for one in sent:
         one.wait_send()
 
@@ -166,7 +174,7 @@
         return ring.copy(hand_out.at[i], hand_in.at[i], hs.at[i], hr.at[i], ring.mate)
 
     def hand_over(i, o):
-        hand_out[i] = partial(ring.chip(-o), 1 - ring.core).astype(BF16)
+        hand_out[i] = partial(i, False, ring.chip(-o), 1 - ring.core).astype(BF16)
         start(hand_copy(i))
 
     def hand_overs(j):
@@ -177,7 +185,7 @@
             hand_over(chips - 1, 0)
 
     def both(i, o):
-        value = partial(ring.chip(o), ring.core)
+        value = partial(i, True, ring.chip(o), ring.core)
         ring.copy(hand_in.at[i], hand_in.at[i], hs.at[i], hr.at[i], ring.mate).wait_recv()
         return value + hand_in[i].astype(F32)
 
@@ -187,7 +195,6 @@
         return ref[...].astype(F32)
 
     hand_overs(0)
-    hand_overs(1)
     for j, now in enumerate(steps):
         for place, (i, o, slot, device, first) in enumerate(now):
             held[place] = both(i, o)
@@ -207,10 +214,10 @@
                         device,
                     )
                 )
+        if j == 0:
+            hand_overs(1)
         hand_overs(j + 2)
         filler(j)
-    if long < 2:
-        hand_overs(long)
     held[0] = both(chips - 1, 0)
     for h in range(2):
         part = pl.ds(h * rows, rows)
@@ -296,19 +303,23 @@
     for load in loads:
         load.wait()
 
-    def normalize(t, carry):
-        part = columns(t, width)
-        x = (blocks[t].astype(F32) * inverse * gain[:, part].astype(F32)).astype(BF16)
-        normed[t] = x
-        factor[...] += dot_t(down[:, part], x)
+    def normalize(q, carry):
+        terms = 0.0
+        for t in (4 * q, 4 * q + 1, 4 * q + 2, 4 * q + 3):
+            part = columns(t, width)
+            scale = gain[part].astype(F32)[None, :] if len(gain.shape) == 1 else gain[:, part]
+            x = (blocks[t].astype(F32) * inverse * scale.astype(F32)).astype(BF16)
+            normed[t] = x
+            terms = terms + dot_t(down[:, part], x)
+        factor[...] += terms
         return carry
 
-    lax.fori_loop(0, n, normalize, 0)
+    lax.fori_loop(0, n // 4, normalize, 0)
     masked = jnp.where(ids[...] == ring.me, factor[...], 0.0).T.astype(BF16)
     own = normed[ring.me]
     devices_a_head = n // KVH
 
-    def partial(chip, core):
+    def partial(i, mine, chip, core):
         head = lax.div(chip * 2, devices_a_head)
         delta = dot(masked, up[:, columns(chip * 2 + core, width)])
         fresh = dot(own, kvw[:, columns(head * 2 + core, HD)])
@@ -368,9 +379,10 @@
     def on_block(slot):
         factor[...] += dot_t(down[:, columns(slot, width)], blocks[slot])
 
-    def base_product(t, carry):
-        base[t] = dot(attended[...], wo[:, columns(t, width)])
-        return carry
+    def base_product(chip, core):
+        return dot(attended[...], wo[:, columns(chip * 2 + core, width)])
+
+    ahead = base.shape[0] // 2
 
     def fill(step):
         if step == 0:
@@ -379,16 +391,24 @@
             return
         if step == 1:
             loads[1].wait()
-            loads[2].wait()
-        part = share(step - 1, ring.long, n)
-        lax.fori_loop(part.start, part.stop, base_product, 0)
+        for item in share(step - 1, 2 * ring.long, 2 * ahead):
+            i, mine = item // 2, item % 2
+            o = ring.long - i // 2 if i % 2 == 0 else i // 2 - ring.short
+            if mine:
+                base[item] = base_product(ring.chip(o), ring.core)
+            else:
+                base[item] = base_product(ring.chip(-o), 1 - ring.core)
 
     gather_blocks(ring, blocks, gs, gr, fill, on_block)
+    loads[2].wait()
     masked = jnp.where(ids[...] == ring.me, factor[...], 0.0).T.astype(BF16)
 
-    def partial(chip, core):
-        t = chip * 2 + core
-        return base[t] + adapter_scale * dot(masked, up[:, columns(t, width)])
+    def partial(i, mine, chip, core):
+        if i < ahead:
+            first = base[2 * i + 1] if mine else base[2 * i]
+        else:
+            first = base_product(chip, core)
+        return first + adapter_scale * dot(masked, up[:, columns(chip * 2 + core, width)])
 
     out[...] = scatter_sum(ring, partial, lambda step: None, *scatter).astype(BF16)
 
@@ -446,7 +466,7 @@
         name="gather_project",
     )(
         hidden_in,
-        norm_gain[None],
+        norm_gain if width % 512 == 0 else norm_gain[None],
         jnp.swapaxes(variant_ids, 0, 1),
         query_base_matrix,
         kv_weight,
@@ -488,7 +508,7 @@
             pltpu.VMEM(out_weight.shape, BF16),
             pltpu.VMEM((rank, depth), BF16),
             pltpu.VMEM((rank, depth), BF16),
-            pltpu.VMEM((n, rows, width), F32),
+            pltpu.VMEM((8, rows, width), F32),
             pltpu.VMEM((rank, rows), F32),
             pltpu.SemaphoreType.DMA((3,)),
             *gather_sems(n),

time: 92.7 us -> 88.4 us (0.954)
  Pallas kernels: 83.9 us -> 81.1 us
  local copies, waits for them, and re-layouts: 5.07 us -> 3.72 us
    pallas_call x1, Pallas kernels: 46.1 us -> 43.9 us  [body(): pl.pallas_call(functools.partial(first_kernel, n), out_shape=[jax.ShapeDt...]
    broadcast_in_dim x1 -> x0, local copies, waits for them, and re-layouts: 1.35 us -> none  [body(): norm_gain[None]]
where the time goes in v3:
time: 88.4 us; the launch traced here: 88.2 us
  Pallas kernels  81.1 us (92%)
  local copies, waits for them, and re-layouts  3.72 us (4%)
  other arithmetic  2.02 us (2%)
  matrix products  1.24 us (1%)
    pallas_call x1, Pallas kernels, body(): pl.pallas_call(functools.partial(first_kernel, n), out_shape=[jax.ShapeDt...  43.9 us
    pallas_call x1, Pallas kernels, body(): pl.pallas_call(functools.partial(second_kernel, n), out_shape=jax.ShapeDt...  37.2 us
    unnamed x4, local copies, waits for them, and re-layouts  2.25 us

profile of v3, /device:TPU:0, one launch (start us, length us, event | category | flops | bytes accessed | tf_op | source)
XLA Modules:
  0.0 88.2 jit_solution(13464528146074641326)
XLA Ops:
  0.0 0.0 copy-start
  0.0 0.8 iota_compare_fusion
  0.8 43.9 %gather_project.1 = (bf16[128,512]{1,0:T(8,128)(2,1)}, bf16[2,128,128]{2,1,0:T(8,128)(2,1)}) custom-call(bf16[128,512]{1,0:T(8,128)(2,1)} %hidden.1, bf16[8192]{0:T(1024)(128)(2,1)} %gain.1, s32[1,128]{1,0:T(1,128)} %bitcast.44, bf16[8192,512]{1,0:T(8,128)(2,1)} %wq_hbm.1, bf16[512,2048]{1,0:T(8,128)(2,1)} %kvw_hbm.1, bf16[64,8192]{1,0:T(8,128)(2,1)} %bitcast.38, ...), custom_call_target="tpu_custom_call" | custom-call | tf_op jit(solution)/shard_map/gather_project/pallas_call | solution.py:441
  44.7 0.9 %reshape.33 = bf16[128,4,128]{2,1,0:T(4,128)(2,1)S(1)} reshape(bf16[128,512]{1,0:T(8,128)(2,1)} %get-tuple-element.7) | data formatting | bytes 262144 | tf_op jit(solution)/shard_map/reshape | solution.py:478
  45.6 0.8 slice_bitcast_fusion
  46.4 0.3 fusion.7
  46.7 0.1 copy.22
  46.8 0.0 copy-done
  46.8 0.5 fusion.12
  47.3 0.1 copy.16
  47.3 0.1 copy.17
  47.5 0.4 fusion.4
  47.9 0.1 copy.18
  47.9 0.1 copy.19
  48.1 0.1 copy.20
  48.2 0.5 fusion.1
  48.7 0.7 copy.27
  49.3 37.2 %gather_output.1 = bf16[128,512]{1,0:T(8,128)(2,1)} custom-call(bf16[128,512]{1,0:T(8,128)(2,1)} %bitcast.42, s32[1,128]{1,0:T(1,128)} %bitcast.45, bf16[512,8192]{1,0:T(8,128)(2,1)} %wo_hbm.1, bf16[64,8192]{1,0:T(8,128)(2,1)} %bitcast.40, bf16[64,8192]{1,0:T(8,128)(2,1)} %bitcast.41), custom_call_target="tpu_custom_call" | custom-call | tf_op jit(solution)/shard_map/gather_output/pallas_call | solution.py:501
  86.6 1.6 %copy.29 = bf16[128,512]{1,0:T(8,128)(2,1)} copy(bf16[128,512]{1,0:T(8,128)(2,1)} %gather_output.1) | data formatting | bytes 262144
  (2 shorter events, 0.0 us)
Async XLA Ops:
  0.0 46.8 %copy-start = (bf16[1,128,16,256]{3,2,1,0:T(8,128)(2,1)S(1)}, bf16[1,128,16,256]{3,2,1,0:T(8,128)(2,1)}, u32[]{:S(2)}) copy-start(bf16[1,128,16,256]{3,2,1,0:T(8,128)(2,1)} %param.23) | copy-start | bytes 3145732

commit v4 on v3

--- a/solution.py
+++ b/solution.py
@@ -256,7 +256,8 @@
     down_hbm,
     up_hbm,
     query,
-    pair,
+    own_score,
+    fresh_value,
     blocks,
     wq,
     kvw,
@@ -339,11 +340,16 @@
         halves.at[ring.core], halves.at[ring.core], fsem.at[0], fsem.at[1], ring.mate
     )
     swap.start()
-    query[...] = (query_sum[...] + adapter_scale * value[:, :width]).astype(BF16)
+    final = (query_sum[...] + adapter_scale * value[:, :width]).astype(BF16)
+    query[...] = final
     swap.wait_send()
     other = halves.at[1 - ring.core]
     ring.copy(other, other, fsem.at[0], fsem.at[1], ring.mate).wait_recv()
-    pair[...] = halves[...]
+    fresh_value[...] = halves[1]
+    key = halves[0].astype(F32)
+    for h in range(width // HD):
+        head = final[:, h * HD : (h + 1) * HD].astype(F32)
+        own_score[:, h : h + 1] = jnp.sum(head * key, axis=1, keepdims=True) * (1.0 / HD**0.5)
 
 
 def second_kernel(
@@ -438,14 +444,15 @@
     params = functools.partial(
         pltpu.CompilerParams, has_side_effects=True, vmem_limit_bytes=VMEM_LIMIT
     )
-    query_vectors, pair = pl.pallas_call(
+    query_vectors, own, fresh_value = pl.pallas_call(
         functools.partial(first_kernel, n),
         out_shape=[
             jax.ShapeDtypeStruct((rows, width), BF16),
-            jax.ShapeDtypeStruct((2, rows, HD), BF16),
+            jax.ShapeDtypeStruct((rows, width // HD), F32),
+            jax.ShapeDtypeStruct((rows, HD), BF16),
         ],
         in_specs=[VM] * 3 + [ANY] * 4,
-        out_specs=[VM] * 2,
+        out_specs=[VM] * 3,
         scratch_shapes=[
             pltpu.VMEM((n, rows, width), BF16),
             pltpu.VMEM(query_base_matrix.shape, BF16),
@@ -473,7 +480,6 @@
         jnp.swapaxes(query_down, 1, 2)[0],
         query_up_factor[0],
     )
-    fresh_key, fresh_value = pair[0], pair[1]
     local_heads = width // HD
     query_heads = query_vectors.reshape(rows, local_heads, HD)
     stored = kv_cache[0]
@@ -483,7 +489,6 @@
     scores = (
         jnp.einsum("rhd,rld->rhl", query_heads, keys, preferred_element_type=F32) * scale
     )
-    own = jnp.einsum("rhd,rd->rh", query_heads, fresh_key, preferred_element_type=F32) * scale
     positions = jnp.arange(stored.shape[1], dtype=jnp.int32)
     live = positions[None, :] < cache_lengths[:, None]
     scores = jnp.where(live[:, None, :], scores, -jnp.inf)

time: 88.4 us -> 89.4 us (1.011)
  other arithmetic: 2.02 us -> 3.69 us
where the time goes in v4:
time: 89.4 us; the launch traced here: 89.1 us
  Pallas kernels  81.2 us (91%)
  other arithmetic  3.69 us (4%)
  local copies, waits for them, and re-layouts  3.19 us (4%)
  matrix products  0.94 us (1%)
    pallas_call x1, Pallas kernels, body(): pl.pallas_call(functools.partial(first_kernel, n), out_shape=[jax.ShapeDt...  44 us
    pallas_call x1, Pallas kernels, body(): pl.pallas_call(functools.partial(second_kernel, n), out_shape=jax.ShapeDt...  37.2 us
    unnamed x4, local copies, waits for them, and re-layouts  2.25 us

profile of v4, /device:TPU:0, one launch (start us, length us, event | category | flops | bytes accessed | tf_op | source)
XLA Modules:
  0.0 89.1 jit_solution(8358665012521207258)
XLA Ops:
  0.0 0.0 copy-start
  0.0 0.8 iota_compare_fusion
  0.8 44.0 %gather_project.1 = (bf16[128,512]{1,0:T(8,128)(2,1)}, f32[128,4]{1,0:T(8,128)}, bf16[128,128]{1,0:T(8,128)(2,1)}) custom-call(bf16[128,512]{1,0:T(8,128)(2,1)} %hidden.1, bf16[8192]{0:T(1024)(128)(2,1)} %gain.1, s32[1,128]{1,0:T(1,128)} %bitcast.21, bf16[8192,512]{1,0:T(8,128)(2,1)} %wq_hbm.1, bf16[512,2048]{1,0:T(8,128)(2,1)} %kvw_hbm.1, ...), custom_call_target="tpu_custom_call" | custom-call | tf_op jit(solution)/shard_map/gather_project/pallas_call | solution.py:447
  44.8 0.9 %reshape.27 = bf16[128,4,128]{2,1,0:T(4,128)(2,1)S(1)} reshape(bf16[128,512]{1,0:T(8,128)(2,1)} %get-tuple-element.8) | data formatting | bytes 262144 | tf_op jit(solution)/shard_map/reshape | solution.py:484
  45.7 0.8 convert_element_type.18
  46.5 0.0 copy-done
  46.5 0.5 fusion.9
  47.0 0.8 max.3
  47.8 0.4 fusion.4
  48.2 0.9 fusion.8
  49.1 0.5 fusion.1
  49.6 0.7 copy.15
  50.3 37.2 %gather_output.1 = bf16[128,512]{1,0:T(8,128)(2,1)} custom-call(bf16[128,512]{1,0:T(8,128)(2,1)} %bitcast.19, s32[1,128]{1,0:T(1,128)} %bitcast.22, bf16[512,8192]{1,0:T(8,128)(2,1)} %wo_hbm.1, bf16[64,8192]{1,0:T(8,128)(2,1)} %bitcast.17, bf16[64,8192]{1,0:T(8,128)(2,1)} %bitcast.18), custom_call_target="tpu_custom_call" | custom-call | tf_op jit(solution)/shard_map/gather_output/pallas_call | solution.py:506
  87.5 1.6 %copy.17 = bf16[128,512]{1,0:T(8,128)(2,1)} copy(bf16[128,512]{1,0:T(8,128)(2,1)} %gather_output.1) | data formatting | bytes 262144
Async XLA Ops:
  0.0 46.5 %copy-start = (bf16[1,128,16,256]{3,2,1,0:T(8,128)(2,1)S(1)}, bf16[1,128,16,256]{3,2,1,0:T(8,128)(2,1)}, u32[]{:S(2)}) copy-start(bf16[1,128,16,256]{3,2,1,0:T(8,128)(2,1)} %param.23) | copy-start | bytes 3145732
